TPU v7x, 32 devices: a whole 2x2x4 slice. The times are simulated.
32 devices in a mesh: energy: 8 (over z, core), layer: 4 (over y, x).
Axes of the slice: x: 2, y: 2, z: 4, core: 2. Of those that a mesh axis runs over, the one named last changes fastest.
Arguments:
- green_local: bfloat16 [4, 16, 384, 2, 384], P('layer', 'energy'), may hold values from -6 to 6
- hopping: bfloat16 [4, 384, 2, 384], P('layer'), may hold values from -0.005859375 to 0.005859375
- coupling: bfloat16 [4, 384, 384], P('layer'), may hold values from -0.25 to 0.25
Outputs:
- green_full: bfloat16 [4, 16, 384, 2, 384], P('layer', 'energy')
All inputs are finite; a program needn't handle non-finite values.
Results may differ from a plain program's by a relative error of at most 0.02.
Values may be sent and summed in bfloat16 or wider, within the bound.
A program may use at most 64 MiB of HBM per device.

v0:
```python
import jax
import jax.numpy as jnp
from jax import lax
from jax.sharding import PartitionSpec as P

OFFSET = 2


def from_behind(value, axis, steps):
    count = lax.axis_size(axis)
    first, last = (max(0, -steps), min(count, count - steps))
    return lax.ppermute(value, axis, [(source, source + steps) for source in range(first, last)])


def padded(array, sides, width):
    for axis, dim in sides:
        size, length = (lax.axis_size(axis), array.shape[dim])
        up = [(i, (i + 1) % size) for i in range(size - 1)]
        down = [(j, i) for i, j in up]
        last = lax.slice_in_dim(array, length - width, length, axis=dim)
        first = lax.slice_in_dim(array, 0, width, axis=dim)
        before = lax.ppermute(last, axis, up)
        after = lax.ppermute(first, axis, down)
        array = jnp.concatenate([before, array, after], axis=dim)
    return array


def expand(blocks):
    real_part = blocks[..., :, 0, :]
    imag_part = blocks[..., :, 1, :]
    upper_half = jnp.concatenate([real_part, imag_part], axis=-1)
    lower_half = jnp.concatenate([-imag_part, real_part], axis=-1)
    return jnp.concatenate([upper_half, lower_half], axis=-2)


def complex_product(left_block, right_block):
    row_blocks = left_block.reshape(left_block.shape[:-2] + (2 * left_block.shape[-1],))
    product_rows = jnp.matmul(row_blocks, expand(right_block), preferred_element_type=jnp.float32)
    return product_rows.reshape(left_block.shape)


def partner_total(extended, energy_count):
    return (
        extended[2 * OFFSET :].astype(jnp.float32) + extended[:energy_count].astype(jnp.float32)
    ).astype(jnp.bfloat16)


def per_device(green_local, hopping, coupling):
    layer_count = lax.axis_size("layer")
    position = lax.axis_index("layer")
    isolated = green_local[0]
    phonon = coupling[0]
    energy_count = isolated.shape[0]
    coupled = complex_product(isolated, hopping[0]).astype(jnp.bfloat16)
    flipped = jnp.transpose(coupled, (0, 3, 2, 1))
    at_top = position == layer_count - 1

    def advance(operands):
        following, partner = operands
        scatter_left = jnp.einsum(
            "ij,ejcl->eicl", phonon, partner, preferred_element_type=jnp.float32
        ).astype(jnp.bfloat16)
        combined = (
            following.astype(jnp.float32)
            + jnp.matmul(scatter_left, phonon.T, preferred_element_type=jnp.float32)
        ).astype(jnp.bfloat16)
        product = complex_product(coupled, combined).astype(jnp.bfloat16)
        return (isolated.astype(jnp.float32) + complex_product(product, flipped)).astype(
            jnp.bfloat16
        )

    result = isolated
    for sweep_step in range(layer_count):
        arrived = from_behind(result, "layer", -1)
        following = jnp.where(at_top, isolated, arrived)
        extended = padded(following, (("energy", 0),), OFFSET)
        partner = partner_total(extended, energy_count)
        active = position == layer_count - 1 - sweep_step
        result = lax.cond(
            active, advance, lambda operands, kept_value=result: kept_value, (following, partner)
        )
    return result[None]


def solution(mesh):
    placed = (
        P("layer", "energy", None, None, None),
        P("layer", None, None, None),
        P("layer", None, None),
    )
    return jax.shard_map(
        per_device,
        mesh=mesh,
        in_specs=placed,
        out_specs=P("layer", "energy", None, None, None),
        check_vma=False,
    )
```

profile of v0, /device:TPU:9, one launch (start us, length us, event | category | flops | bytes accessed | tf_op | source)
XLA Modules:
  0.0 321.9 jit_solution(6030373129330487075)
XLA Ops:
  0.0 3.6 %copy.11 = bf16[2,384,2,384]{1,3,2,0:T(8,128)(2,1)S(1)} copy(bf16[2,384,2,384]{3,2,1,0:T(2,128)(2,1)} %bitcast.133) | data formatting | bytes 2359296 | tf_op jit(solution)/shard_map/squeeze | solution.py:51
  3.6 1.4 collective-permute-start
  5.0 27.4 %collective-permute-done = bf16[2,384,2,384]{1,3,2,0:T(8,128)(2,1)S(1)} collective-permute-done((bf16[2,384,2,384]{1,3,2,0:T(8,128)(2,1)S(1)}, bf16[2,384,2,384]{1,3,2,0:T(8,128)(2,1)S(1)}, u32[]{:S(2)}, u32[]{:S(2)}) %collective-permute-start) | collective-permute-done | bytes 1179680 | tf_op jit(solution)/shard_map/ppermute | solution.py:12
  32.5 1.2 broadcast_select_fusion.3
  33.6 3.6 %collective-permute-start.1 = (bf16[2,384,2,384]{1,3,2,0:T(8,128)(2,1)}, bf16[2,384,2,384]{1,3,2,0:T(8,128)(2,1)}, u32[]{:S(2)}, u32[]{:S(2)}) collective-permute-start(bf16[2,384,2,384]{1,3,2,0:T(8,128)(2,1)} %broadcast_select_fusion.3), channel_id=1, source_target_pairs={{4,0},{8,4},{12,8},{16,12},{20,16},{24,20},{28,24},{5,1},{9,5},{13... | collective-permute-start | bytes 3538952 | tf_op jit(solution)/shard_map/ppermute | solution.py:23
  37.2 3.1 collective-permute-start.2
  40.3 1.6 reshape_squeeze.3
  41.9 1.0 copy.12
  43.0 3.4 %convolution_convert_fusion.4 = bf16[768,2,384]{2,0,1:T(8,128)(2,1)} fusion(bf16[2,384,768]{2,1,0:T(8,128)(2,1)} %reshape_squeeze.3, bf16[384,384]{0,1:T(8,128)(2,1)S(1)} %get-tuple-element.137, bf16[384,384]{0,1:T(8,128)(2,1)S(1)} %fusion.122, bf16[384,384]{0,1:T(8,128)(2,1)S(1)} %get-tuple-element.136), kind=kOutput, calls=%fused_computation.122 | convolution fusion | flops 911278080 | bytes 3244032 | tf_op jit(solution)/shard_map/dot_general | solution.py:38
  46.5 1.4 copy.49
  47.9 5.0 %collective-permute-done.1 = bf16[2,384,2,384]{1,3,2,0:T(8,128)(2,1)} collective-permute-done((bf16[2,384,2,384]{1,3,2,0:T(8,128)(2,1)}, bf16[2,384,2,384]{1,3,2,0:T(8,128)(2,1)}, u32[]{:S(2)}, u32[]{:S(2)}) %collective-permute-start.1) | collective-permute-done | bytes 1179680 | tf_op jit(solution)/shard_map/ppermute | solution.py:23
  52.9 0.9 collective-permute-done.2
  53.7 2.9 add_convert_fusion.11
  56.7 1.1 conditional.4
  56.7 1.1 copy.50
  57.8 4.7 %copy.16 = bf16[2,384,2,384]{1,3,2,0:T(8,128)(2,1)} copy(bf16[2,384,2,384]{3,2,1,0:T(2,128)(2,1)} %get-tuple-element.140) | data formatting | bytes 2359296 | tf_op jit(solution)/shard_map/cond | solution.py:79
  62.5 1.3 collective-permute-start.3
  63.8 27.9 %collective-permute-done.3 = bf16[2,384,2,384]{1,3,2,0:T(8,128)(2,1)S(1)} collective-permute-done((bf16[2,384,2,384]{1,3,2,0:T(8,128)(2,1)}, bf16[2,384,2,384]{1,3,2,0:T(8,128)(2,1)S(1)}, u32[]{:S(2)}, u32[]{:S(2)}) %collective-permute-start.3) | collective-permute-done | bytes 1179680 | tf_op jit(solution)/shard_map/ppermute | solution.py:12
  91.7 1.2 broadcast_select_fusion.2
  92.9 3.8 %collective-permute-start.4 = (bf16[2,384,2,384]{1,3,2,0:T(8,128)(2,1)}, bf16[2,384,2,384]{1,3,2,0:T(8,128)(2,1)}, u32[]{:S(2)}, u32[]{:S(2)}) collective-permute-start(bf16[2,384,2,384]{1,3,2,0:T(8,128)(2,1)} %broadcast_select_fusion.2), channel_id=1, source_target_pairs={{4,0},{8,4},{12,8},{16,12},{20,16},{24,20},{28,24},{5,1},{9,5},{13... | collective-permute-start | bytes 3538952 | tf_op jit(solution)/shard_map/ppermute | solution.py:23
  96.7 3.1 collective-permute-start.5
  99.8 12.5 %collective-permute-done.4 = bf16[2,384,2,384]{1,3,2,0:T(8,128)(2,1)} collective-permute-done((bf16[2,384,2,384]{1,3,2,0:T(8,128)(2,1)}, bf16[2,384,2,384]{1,3,2,0:T(8,128)(2,1)}, u32[]{:S(2)}, u32[]{:S(2)}) %collective-permute-start.4) | collective-permute-done | bytes 1179680 | tf_op jit(solution)/shard_map/ppermute | solution.py:23
  113.3 2.9 add_convert_fusion.10
  116.2 4.7 %copy.20 = bf16[2,384,2,384]{1,3,2,0:T(8,128)(2,1)} copy(bf16[2,384,2,384]{3,2,1,0:T(2,128)(2,1)} %get-tuple-element.141) | data formatting | bytes 2359296 | tf_op jit(solution)/shard_map/cond | solution.py:79
  121.0 1.3 collective-permute-start.6
  122.2 28.1 %collective-permute-done.6 = bf16[2,384,2,384]{1,3,2,0:T(8,128)(2,1)S(1)} collective-permute-done((bf16[2,384,2,384]{1,3,2,0:T(8,128)(2,1)}, bf16[2,384,2,384]{1,3,2,0:T(8,128)(2,1)S(1)}, u32[]{:S(2)}, u32[]{:S(2)}) %collective-permute-start.6) | collective-permute-done | bytes 1179680 | tf_op jit(solution)/shard_map/ppermute | solution.py:12
  150.4 1.2 broadcast_select_fusion.1
  151.5 3.8 %collective-permute-start.7 = (bf16[2,384,2,384]{1,3,2,0:T(8,128)(2,1)}, bf16[2,384,2,384]{1,3,2,0:T(8,128)(2,1)}, u32[]{:S(2)}, u32[]{:S(2)}) collective-permute-start(bf16[2,384,2,384]{1,3,2,0:T(8,128)(2,1)} %broadcast_select_fusion.1), channel_id=1, source_target_pairs={{4,0},{8,4},{12,8},{16,12},{20,16},{24,20},{28,24},{5,1},{9,5},{13... | collective-permute-start | bytes 3538952 | tf_op jit(solution)/shard_map/ppermute | solution.py:23
  155.4 1.9 collective-permute-start.8
  157.3 12.5 %collective-permute-done.7 = bf16[2,384,2,384]{1,3,2,0:T(8,128)(2,1)} collective-permute-done((bf16[2,384,2,384]{1,3,2,0:T(8,128)(2,1)}, bf16[2,384,2,384]{1,3,2,0:T(8,128)(2,1)}, u32[]{:S(2)}, u32[]{:S(2)}) %collective-permute-start.7) | collective-permute-done | bytes 1179680 | tf_op jit(solution)/shard_map/ppermute | solution.py:23
  170.8 2.9 add_convert_fusion.9
  173.7 4.7 %copy.24 = bf16[2,384,2,384]{1,3,2,0:T(8,128)(2,1)} copy(bf16[2,384,2,384]{3,2,1,0:T(2,128)(2,1)} %get-tuple-element.142) | data formatting | bytes 2359296 | tf_op jit(solution)/shard_map/cond | solution.py:79
  178.4 1.5 collective-permute-start.9
  179.9 91.5 %collective-permute-done.9 = bf16[2,384,2,384]{1,3,2,0:T(8,128)(2,1)S(1)} collective-permute-done((bf16[2,384,2,384]{1,3,2,0:T(8,128)(2,1)}, bf16[2,384,2,384]{1,3,2,0:T(8,128)(2,1)S(1)}, u32[]{:S(2)}, u32[]{:S(2)}) %collective-permute-start.9) | collective-permute-done | bytes 1179680 | tf_op jit(solution)/shard_map/ppermute | solution.py:12
  271.5 1.2 broadcast_select_fusion
  272.6 4.8 %copy.26 = bf16[2,384,2,384]{3,2,1,0:T(2,128)(2,1)} copy(bf16[2,384,2,384]{1,3,2,0:T(8,128)(2,1)} %broadcast_select_fusion) | data formatting | bytes 2359296 | tf_op jit(solution)/shard_map/jit(_where)/select_n | solution.py:75
  277.4 5.2 %collective-permute-start.10 = (bf16[2,384,2,384]{3,2,1,0:T(2,128)(2,1)}, bf16[2,384,2,384]{3,2,1,0:T(2,128)(2,1)}, u32[]{:S(2)}, u32[]{:S(2)}) collective-permute-start(bf16[2,384,2,384]{3,2,1,0:T(2,128)(2,1)} %copy.26), channel_id=1, source_target_pairs={{4,0},{8,4},{12,8},{16,12},{20,16},{24,20},{28,24},{5,1},{9,5},{13... | collective-permute-start | bytes 3538952 | tf_op jit(solution)/shard_map/ppermute | solution.py:23
  282.5 1.9 collective-permute-start.11
  284.5 12.5 %collective-permute-done.10 = bf16[2,384,2,384]{3,2,1,0:T(2,128)(2,1)} collective-permute-done((bf16[2,384,2,384]{3,2,1,0:T(2,128)(2,1)}, bf16[2,384,2,384]{3,2,1,0:T(2,128)(2,1)}, u32[]{:S(2)}, u32[]{:S(2)}) %collective-permute-start.10) | collective-permute-done | bytes 1179680 | tf_op jit(solution)/shard_map/ppermute | solution.py:23
  297.9 3.9 %add_convert_fusion.8 = bf16[2,384,2,384]{3,2,1,0:T(2,128)(2,1)} fusion(bf16[2,384,2,384]{3,2,1,0:T(2,128)(2,1)} %collective-permute-done.11, bf16[2,384,2,384]{3,2,1,0:T(2,128)(2,1)} %collective-permute-done.10), kind=kLoop, calls=%fused_computation.118 | loop fusion | flops 2359296 | bytes 3538944 | tf_op jit(solution)/shard_map/convert_element_type | solution.py:45
  301.8 19.1 %conditional.7 = (bf16[1,2,384,2,384]{4,3,2,1,0:T(2,128)(2,1)S(1)}) conditional(s32[]{:T(128)} %convert_element_type.149, bf16[2,384,2,384]{3,2,1,0:T(2,128)(2,1)S(1)} %copy-done.1, (bf16[2,384,2,384]{3,2,1,0:T(2,128)(2,1)S(1)}, bf16[2,384,2,384]{1,3,2,0:T(8,128)(2,1)}, bf16[2,384,2,384]{3,2,1,0:T(2,128)(2,1)}, bf16[384,384]{1,0:T(8,128)(2,1)}, ...), branch_computations={%region_6.7_spmd, %region_7.8_spmd} | conditional | flops 2742091776 | bytes 27426824 | solution.py:79
  301.8 3.2 add_convert_fusion.7
  305.0 1.1 slice_bitcast_fusion.12
  306.1 1.1 slice_bitcast_fusion.14
  308.2 6.0 %fusion.92 = f32[2,384,768]{2,1,0:T(8,128)} fusion(bf16[2,384,384]{2,1,0:T(8,128)(2,1)} %get-tuple-element.135, bf16[2,384,384]{2,1,0:T(8,128)(2,1)S(1)} %fusion.113, bf16[2,384,384]{2,1,0:T(8,128)(2,1)} %get-tuple-element.134, bf16[2,384,768]{1,2,0:T(8,128)(2,1)} %bitcast.30, bf16[2,384,384]{1,2,0:T(8,128)(2,1)} %get-tuple-element.133, ...), kind=kOutput, calls=%fused_computation.95 | convolution fusion | flops 1831403520 | bytes 7077888 | tf_op jit(solution)/shard_map/cond/branch_1_fun/dot_general | solution.py:38
  314.2 3.9 %reshape.28 = f32[2,384,2,384]{3,2,1,0:T(2,128)} reshape(f32[2,384,768]{2,1,0:T(8,128)} %fusion.92) | data formatting | bytes 4718592 | tf_op jit(solution)/shard_map/cond/branch_1_fun/reshape | solution.py:39
  318.0 2.9 fusion.104
  320.9 1.0 copy-done.2
  (16 shorter events, 3.7 us)
Async XLA Ops:
  3.6 36.7 %copy-start = (bf16[1,2,384,2,384]{4,3,2,1,0:T(2,128)(2,1)S(1)}, bf16[1,2,384,2,384]{4,3,2,1,0:T(2,128)(2,1)}, u32[]{:S(2)}) copy-start(bf16[1,2,384,2,384]{4,3,2,1,0:T(2,128)(2,1)} %param.11) | copy-start | bytes 3538948
  3.6 28.9 %collective-permute-start = (bf16[2,384,2,384]{1,3,2,0:T(8,128)(2,1)S(1)}, bf16[2,384,2,384]{1,3,2,0:T(8,128)(2,1)S(1)}, u32[]{:S(2)}, u32[]{:S(2)}) collective-permute-start(bf16[2,384,2,384]{1,3,2,0:T(8,128)(2,1)S(1)} %copy.11), channel_id=1, source_target_pairs={{1,0},{2,1},{3,2},{5,4},{6,5},{7,6},{9,8},{10,9},{11,10},{13,12},{... | collective-permute-start | bytes 3538952 | tf_op jit(solution)/shard_map/ppermute | solution.py:12
  33.6 8.3 %copy-start.6 = (bf16[1,384,2,384]{3,2,1,0:T(2,128)(2,1)S(1)}, bf16[1,384,2,384]{3,2,1,0:T(2,128)(2,1)}, u32[]{:S(2)}) copy-start(bf16[1,384,2,384]{3,2,1,0:T(2,128)(2,1)} %param.12) | copy-start | bytes 1769476
  33.6 19.2 %collective-permute-start.1 = (bf16[2,384,2,384]{1,3,2,0:T(8,128)(2,1)}, bf16[2,384,2,384]{1,3,2,0:T(8,128)(2,1)}, u32[]{:S(2)}, u32[]{:S(2)}) collective-permute-start(bf16[2,384,2,384]{1,3,2,0:T(8,128)(2,1)} %broadcast_select_fusion.3), channel_id=1, source_target_pairs={{4,0},{8,4},{12,8},{16,12},{20,16},{24,20},{28,24},{5,1},{9,5},{13... | collective-permute-start | bytes 3538952 | tf_op jit(solution)/shard_map/ppermute | solution.py:23
  37.2 16.6 %collective-permute-start.2 = (bf16[2,384,2,384]{1,3,2,0:T(8,128)(2,1)}, bf16[2,384,2,384]{1,3,2,0:T(8,128)(2,1)}, u32[]{:S(2)}, u32[]{:S(2)}) collective-permute-start(bf16[2,384,2,384]{1,3,2,0:T(8,128)(2,1)} %broadcast_select_fusion.3), channel_id=1, source_target_pairs={{0,4},{4,8},{8,12},{12,16},{16,20},{20,24},{24,28},{1,5},{5,9},{9,... | collective-permute-start | bytes 3538952 | tf_op jit(solution)/shard_map/ppermute | solution.py:22
  62.5 29.2 %collective-permute-start.3 = (bf16[2,384,2,384]{1,3,2,0:T(8,128)(2,1)}, bf16[2,384,2,384]{1,3,2,0:T(8,128)(2,1)S(1)}, u32[]{:S(2)}, u32[]{:S(2)}) collective-permute-start(bf16[2,384,2,384]{1,3,2,0:T(8,128)(2,1)} %copy.16), channel_id=1, source_target_pairs={{1,0},{2,1},{3,2},{5,4},{6,5},{7,6},{9,8},{10,9},{11,10},{13,12},{... | collective-permute-start | bytes 3538952 | tf_op jit(solution)/shard_map/ppermute | solution.py:12
  92.9 19.5 %collective-permute-start.4 = (bf16[2,384,2,384]{1,3,2,0:T(8,128)(2,1)}, bf16[2,384,2,384]{1,3,2,0:T(8,128)(2,1)}, u32[]{:S(2)}, u32[]{:S(2)}) collective-permute-start(bf16[2,384,2,384]{1,3,2,0:T(8,128)(2,1)} %broadcast_select_fusion.2), channel_id=1, source_target_pairs={{4,0},{8,4},{12,8},{16,12},{20,16},{24,20},{28,24},{5,1},{9,5},{13... | collective-permute-start | bytes 3538952 | tf_op jit(solution)/shard_map/ppermute | solution.py:23
  96.7 16.6 %collective-permute-start.5 = (bf16[2,384,2,384]{1,3,2,0:T(8,128)(2,1)}, bf16[2,384,2,384]{1,3,2,0:T(8,128)(2,1)}, u32[]{:S(2)}, u32[]{:S(2)}) collective-permute-start(bf16[2,384,2,384]{1,3,2,0:T(8,128)(2,1)} %broadcast_select_fusion.2), channel_id=1, source_target_pairs={{0,4},{4,8},{8,12},{12,16},{16,20},{20,24},{24,28},{1,5},{5,9},{9,... | collective-permute-start | bytes 3538952 | tf_op jit(solution)/shard_map/ppermute | solution.py:22
  121.0 29.4 %collective-permute-start.6 = (bf16[2,384,2,384]{1,3,2,0:T(8,128)(2,1)}, bf16[2,384,2,384]{1,3,2,0:T(8,128)(2,1)S(1)}, u32[]{:S(2)}, u32[]{:S(2)}) collective-permute-start(bf16[2,384,2,384]{1,3,2,0:T(8,128)(2,1)} %copy.20), channel_id=1, source_target_pairs={{1,0},{2,1},{3,2},{5,4},{6,5},{7,6},{9,8},{10,9},{11,10},{13,12},{... | collective-permute-start | bytes 3538952 | tf_op jit(solution)/shard_map/ppermute | solution.py:12
  151.5 18.3 %collective-permute-start.7 = (bf16[2,384,2,384]{1,3,2,0:T(8,128)(2,1)}, bf16[2,384,2,384]{1,3,2,0:T(8,128)(2,1)}, u32[]{:S(2)}, u32[]{:S(2)}) collective-permute-start(bf16[2,384,2,384]{1,3,2,0:T(8,128)(2,1)} %broadcast_select_fusion.1), channel_id=1, source_target_pairs={{4,0},{8,4},{12,8},{16,12},{20,16},{24,20},{28,24},{5,1},{9,5},{13... | collective-permute-start | bytes 3538952 | tf_op jit(solution)/shard_map/ppermute | solution.py:23
  155.4 15.4 %collective-permute-start.8 = (bf16[2,384,2,384]{1,3,2,0:T(8,128)(2,1)}, bf16[2,384,2,384]{1,3,2,0:T(8,128)(2,1)}, u32[]{:S(2)}, u32[]{:S(2)}) collective-permute-start(bf16[2,384,2,384]{1,3,2,0:T(8,128)(2,1)} %broadcast_select_fusion.1), channel_id=1, source_target_pairs={{0,4},{4,8},{8,12},{12,16},{16,20},{20,24},{24,28},{1,5},{5,9},{9,... | collective-permute-start | bytes 3538952 | tf_op jit(solution)/shard_map/ppermute | solution.py:22
  178.4 93.0 %collective-permute-start.9 = (bf16[2,384,2,384]{1,3,2,0:T(8,128)(2,1)}, bf16[2,384,2,384]{1,3,2,0:T(8,128)(2,1)S(1)}, u32[]{:S(2)}, u32[]{:S(2)}) collective-permute-start(bf16[2,384,2,384]{1,3,2,0:T(8,128)(2,1)} %copy.24), channel_id=1, source_target_pairs={{1,0},{2,1},{3,2},{5,4},{6,5},{7,6},{9,8},{10,9},{11,10},{13,12},{... | collective-permute-start | bytes 3538952 | tf_op jit(solution)/shard_map/ppermute | solution.py:12
  277.4 24.4 %copy-start.1 = (bf16[2,384,2,384]{3,2,1,0:T(2,128)(2,1)S(1)}, bf16[2,384,2,384]{3,2,1,0:T(2,128)(2,1)}, u32[]{:S(2)}) copy-start(bf16[2,384,2,384]{3,2,1,0:T(2,128)(2,1)} %get-tuple-element.142) | copy-start | bytes 3538948
  277.4 19.6 %collective-permute-start.10 = (bf16[2,384,2,384]{3,2,1,0:T(2,128)(2,1)}, bf16[2,384,2,384]{3,2,1,0:T(2,128)(2,1)}, u32[]{:S(2)}, u32[]{:S(2)}) collective-permute-start(bf16[2,384,2,384]{3,2,1,0:T(2,128)(2,1)} %copy.26), channel_id=1, source_target_pairs={{4,0},{8,4},{12,8},{16,12},{20,16},{24,20},{28,24},{5,1},{9,5},{13... | collective-permute-start | bytes 3538952 | tf_op jit(solution)/shard_map/ppermute | solution.py:23
  282.5 15.4 %collective-permute-start.11 = (bf16[2,384,2,384]{3,2,1,0:T(2,128)(2,1)}, bf16[2,384,2,384]{3,2,1,0:T(2,128)(2,1)}, u32[]{:S(2)}, u32[]{:S(2)}) collective-permute-start(bf16[2,384,2,384]{3,2,1,0:T(2,128)(2,1)} %copy.26), channel_id=1, source_target_pairs={{0,4},{4,8},{8,12},{12,16},{16,20},{20,24},{24,28},{1,5},{5,9},{9,... | collective-permute-start | bytes 3538952 | tf_op jit(solution)/shard_map/ppermute | solution.py:22
  320.9 1.0 copy-start.2
where the time goes:
time: 325 us; the launch traced here: 322 us
  waiting for transfers between devices  221 us (68%)
  local copies, waits for them, and re-layouts  34.8 us (11%)
  starting transfers between devices  31.9 us (10%)
  other arithmetic  21.1 us (6%)
  matrix products  12.6 us (4%)
    ppermute x4, waiting for transfers between devices, from_behind(): lax.ppermute(value, axis, [(source, source + steps) for source in range(f...  175 us
    ppermute x4, waiting for transfers between devices, padded(): after = lax.ppermute(first, axis, down)  42.7 us
    ppermute x4, starting transfers between devices, padded(): after = lax.ppermute(first, axis, down)  16.4 us
    cond x3, local copies, waits for them, and re-layouts, per_device(): lax.cond(active, advance, lambda operands, kept_value=result: kept_value,...  14.2 us
    convert_element_type x4, other arithmetic, partner_total(): return (extended[2 * OFFSET:].astype(jnp.float32) + extended[:energy_coun...  12.7 us
    ppermute x4, starting transfers between devices, padded(): before = lax.ppermute(last, axis, up)  10.1 us
    dot_general x2, matrix products, complex_product(): jnp.matmul(row_blocks, expand(right_block), preferred_element_type=jnp.fl...  9.43 us
  transfers between devices with their start and end apart: 12, of which 12 were waited for; matrix products, arithmetic and copies ran while one was open for 2% of the time, Pallas kernels for 0%

commit v1 on v0

v1 whole, which is shorter than its diff:
```python
import functools

import jax
import jax.numpy as jnp
from jax import lax
from jax.experimental import pallas as pl
from jax.experimental.pallas import tpu as pltpu
from jax.sharding import PartitionSpec as P

MESH = pl.DeviceIdType.MESH
F32 = jnp.float32
BF16 = jnp.bfloat16


def routes(layers, energies):
    if layers == 4 and energies == 2:
        return [
            (0, (3, 2)),
            (1, (3, 1, 0, 2)),
            (0, (2, 3, 1)),
            (1, (2, 0, 1)),
            (0, (1, 0)),
            (1, (1, 3, 2, 0)),
        ]
    return [(i, (l, l - 1)) for l in range(layers - 1, 0, -1) for i in range(energies)]


def kernel(
    dims, streams, slots,
    g_ref, h_ref, c_ref, out_ref,
    fin, halo, relay, right, left, mid,
    fin_sem, halo_sem, relay_sem, out_send, halo_send, relay_send,
):
    layers, rows_of, energies, chunks, rows, size, group = dims
    me = lax.axis_index("layer")
    d = lax.axis_index("energy")
    has_low, has_high = d > 0, d < rows_of - 1
    top = me == layers - 1

    pairs = sorted({tuple(sorted(p)) for _, path in streams for p in zip(path, path[1:])})
    barrier = pltpu.get_barrier_semaphore()
    count = has_low.astype(jnp.int32) + has_high.astype(jnp.int32)
    for l in range(layers):
        partners = [b if a == l else a for a, b in pairs if l in (a, b)]

        @pl.when(me == l)
        def _(partners=partners):
            for other in partners:
                pl.semaphore_signal(barrier, inc=1, device_id={"layer": other}, device_id_type=MESH)

        count = count + jnp.where(me == l, len(partners), 0)

    @pl.when(has_low)
    def _():
        pl.semaphore_signal(barrier, inc=1, device_id={"energy": d - 1}, device_id_type=MESH)

    @pl.when(has_high)
    def _():
        pl.semaphore_signal(barrier, inc=1, device_id={"energy": d + 1}, device_id_type=MESH)

    pl.semaphore_wait(barrier, count)

    def halo_copy(src, side, i, c):
        return pltpu.make_async_remote_copy(
            src_ref=src.at[i, c], dst_ref=halo.at[side, i, c],
            send_sem=halo_send.at[side, i, c], recv_sem=halo_sem.at[side, i, c],
            device_id={"energy": d + 1 if side == 0 else d - 1}, device_id_type=MESH,
        )

    def forward(src, i, c):
        @pl.when(has_high)
        def _():
            halo_copy(src, 0, i, c).start()

        @pl.when(has_low)
        def _():
            halo_copy(src, 1, i, c).start()

    def stream_copy(s, hop, c):
        i, path = streams[s]
        target = path[hop + 1]
        if hop == 0:
            src, send = out_ref.at[i, c], out_send.at[i, c]
        else:
            src, send = relay.at[slots[s], c], relay_send.at[slots[s], c]
        if hop == len(path) - 2:
            dst, recv = fin.at[i, c], fin_sem.at[i, c]
        else:
            dst, recv = relay.at[slots[s], c], relay_sem.at[slots[s], c]
        return pltpu.make_async_remote_copy(
            src_ref=src, dst_ref=dst, send_sem=send, recv_sem=recv,
            device_id={"layer": target}, device_id_type=MESH,
        )

    def pass_on(s, hop):
        def body(c, carry):
            stream_copy(s, hop - 1, c).wait_recv()
            stream_copy(s, hop, c).start()
            return carry

        lax.fori_loop(0, chunks, body, 0)

    @pl.when(top)
    def _():
        def body(c, carry):
            for i in range(energies):
                forward(g_ref, i, c)
            return carry

        lax.fori_loop(0, chunks, body, 0)
        fin[...] = g_ref[...]

    @pl.when(d == 0)
    def _():
        halo[0] = jnp.zeros_like(halo[0])

    @pl.when(d == rows_of - 1)
    def _():
        halo[1] = jnp.zeros_like(halo[1])

    hop_r, hop_i = h_ref[:, :size], h_ref[:, size:]
    mid[0, :size, :] = h_ref[...]
    mid[0, size : 2 * size, :size] = -hop_i
    mid[0, size : 2 * size, size:] = hop_r
    for i in range(energies):
        blocks = g_ref[i].reshape(size, 2 * size)
        left[i, :, : 2 * size] = jnp.dot(
            blocks, mid[0, : 2 * size, :], preferred_element_type=F32
        ).astype(BF16)
    for i in range(energies):
        for part in range(2):
            factor = left[i, :, part * size : (part + 1) * size]
            left[i, :, (2 + part) * size : (3 + part) * size] = jnp.dot(
                factor, c_ref[...], preferred_element_type=F32
            ).astype(BF16)
        for which in range(2):
            start = 2 * which * size
            flip_r = left[i, :, start : start + size].T
            flip_i = left[i, :, start + size : start + 2 * size].T
            right[i, which, :size, :size] = flip_r
            right[i, which, :size, size:] = flip_i
            right[i, which, size:, :size] = -flip_i
            right[i, which, size:, size:] = flip_r

    def relays(when):
        for l in range(layers):
            jobs = [
                (s, hop)
                for s, (_, path) in enumerate(streams)
                for hop, node in enumerate(path[1:-1], 1)
                if node == l and (path[0] > l + 1 if when == "before" else path[0] <= l)
            ]
            if jobs:
                @pl.when(me == l)
                def _(jobs=jobs):
                    for s, hop in jobs:
                        pass_on(s, hop)

    relays("before")

    def expand_into(i, which, c, value):
        value = value.astype(BF16)
        base = which * 2 * size + c * rows
        mid[i, pl.ds(pl.multiple_of(base, 16), rows), :] = value
        low = pl.ds(pl.multiple_of(base + size, 16), rows)
        mid[i, low, :size] = -value[:, size:]
        mid[i, low, size:] = value[:, :size]

    lags = []
    for i in range(energies):
        lag = jnp.int32(0)
        for l in range(layers - 1):
            hops = {e: len(path) for e, path in streams if path[-1] == l}
            lag = lag + jnp.where(me == l, hops[i] - min(hops.values()), 0)
        lags.append(lag)
    worst = max(len(path) for _, path in streams) - 2

    def step(t, carry):
        for i in range(energies):
            c = t - lags[i]

            @pl.when((c >= 0) & (c < chunks) & jnp.logical_not(top))
            def _(i=i, c=c):
                pltpu.make_async_remote_copy(
                    src_ref=fin.at[i, c], dst_ref=fin.at[i, c],
                    send_sem=out_send.at[i, c], recv_sem=fin_sem.at[i, c],
                    device_id={"layer": me + 1}, device_id_type=MESH,
                ).wait_recv()
                forward(fin, i, c)

        for i in range(energies):
            c = t - lags[i]

            @pl.when((c >= 0) & (c < chunks))
            def _(i=i, c=c):
                expand_into(i, 0, c, jnp.dot(fin[i, c], right[i, 0], preferred_element_type=F32))

        for i in range(energies):
            c = t - lags[i] - 1

            @pl.when((c >= 0) & (c < chunks))
            def _(i=i, c=c):
                @pl.when(has_low)
                def _():
                    halo_copy(fin, 0, i, c).wait_recv()

                @pl.when(has_high)
                def _():
                    halo_copy(fin, 1, i, c).wait_recv()

                partner = (halo[0, i, c].astype(F32) + halo[1, i, c].astype(F32)).astype(BF16)
                expand_into(i, 1, c, jnp.dot(partner, right[i, 1], preferred_element_type=F32))

        return carry

    lax.fori_loop(0, chunks + 1 + worst, step, 0)

    def finish(k, carry):
        for i in range(energies):
            base = pl.multiple_of(k * (group * rows), 16)
            total = jnp.dot(
                left[i, pl.ds(base, group * rows), :], mid[i], preferred_element_type=F32
            )
            for j in range(group):
                c = k * group + j
                out_ref[i, c] = (
                    g_ref[i, c].astype(F32) + total[j * rows : (j + 1) * rows]
                ).astype(BF16)
            for s, (e, path) in enumerate(streams):
                if e == i:
                    @pl.when(me == path[0])
                    def _(s=s):
                        for j in range(group):
                            stream_copy(s, 0, k * group + j).start()
        return carry

    lax.fori_loop(0, chunks // group, finish, 0)
    relays("after")

    def drain(c, carry):
        for s, (_, path) in enumerate(streams):
            for hop, node in enumerate(path[:-1]):
                @pl.when(me == node)
                def _(s=s, hop=hop):
                    stream_copy(s, hop, c).wait_send()
        for i in range(energies):
            @pl.when(has_high)
            def _(i=i):
                halo_copy(fin, 0, i, c).wait_send()

            @pl.when(has_low)
            def _(i=i):
                halo_copy(fin, 1, i, c).wait_send()
        return carry

    lax.fori_loop(0, chunks, drain, 0)


def per_device(green_local, hopping, coupling):
    _, energies, size, _, _ = green_local.shape
    layers, rows_of = lax.axis_size("layer"), lax.axis_size("energy")
    rows = 64 if size % 64 == 0 else 16
    chunks = size // rows
    group = 2 if chunks % 2 == 0 else 1
    streams = routes(layers, energies)
    slots, relayed = {}, 0
    for s, (_, path) in enumerate(streams):
        if len(path) > 2:
            slots[s] = relayed
            relayed += 1
    relayed = max(relayed, 1)
    block = (energies, chunks, rows, 2 * size)
    sem = pltpu.SemaphoreType.DMA
    vmem = pl.BlockSpec(memory_space=pltpu.VMEM)
    result = pl.pallas_call(
        functools.partial(
            kernel, (layers, rows_of, energies, chunks, rows, size, group), streams, slots
        ),
        out_shape=jax.ShapeDtypeStruct(block, BF16),
        in_specs=[vmem] * 3,
        out_specs=vmem,
        scratch_shapes=[
            pltpu.VMEM(block, BF16),
            pltpu.VMEM((2,) + block, BF16),
            pltpu.VMEM((relayed,) + block[1:], BF16),
            pltpu.VMEM((energies, 2, 2 * size, 2 * size), BF16),
            pltpu.VMEM((energies, size, 4 * size), BF16),
            pltpu.VMEM((energies, 4 * size, 2 * size), BF16),
            sem((energies, chunks)),
            sem((2, energies, chunks)),
            sem((relayed, chunks)),
            sem((energies, chunks)),
            sem((2, energies, chunks)),
            sem((relayed, chunks)),
        ],
        compiler_params=pltpu.CompilerParams(
            collective_id=0, has_side_effects=True, vmem_limit_bytes=48 * 2**20
        ),
        name="sweep",
    )(
        green_local.reshape(block),
        hopping.reshape(size, 2 * size),
        coupling.reshape(size, size),
    )
    return result.reshape(green_local.shape)


def solution(mesh):
    placed = (
        P("layer", "energy", None, None, None),
        P("layer", None, None, None),
        P("layer", None, None),
    )
    return jax.shard_map(
        per_device,
        mesh=mesh,
        in_specs=placed,
        out_specs=P("layer", "energy", None, None, None),
        check_vma=False,
    )
```

time: 325 us -> 108 us (0.33)
  waiting for transfers between devices: 221 us -> 0 us
  Pallas kernels: 0 us -> 103 us
  starting transfers between devices: 31.9 us -> 0 us
  local copies, waits for them, and re-layouts: 34.8 us -> 3.56 us
  other arithmetic: 21.1 us -> 0 us
  matrix products: 12.6 us -> 0 us
    ppermute x12 -> x0, waiting for transfers between devices: 221 us -> none  [the longest x4 175 us: from_behind(): lax.ppermute(value, axis, [(source, source + steps) for source in range(f...]
    pallas_call x0 -> x1, Pallas kernels: none -> 103 us  [per_device(): pl.pallas_call(functools.partial(kernel, (layers, rows_of, energies, chun...]
    ppermute x12 -> x0, starting transfers between devices: 31.9 us -> none  [the longest x4 16.4 us: padded(): after = lax.ppermute(first, axis, down)]
    cond x4 -> x0, local copies, waits for them, and re-layouts: 15.3 us -> none  [the longest x3 14.2 us: per_device(): lax.cond(active, advance, lambda operands, kept_value=result: kept_value,...]
    convert_element_type x4 -> x0, other arithmetic: 12.7 us -> none  [partner_total(): return (extended[2 * OFFSET:].astype(jnp.float32) + extended[:energy_coun...]
    dot_general x3 -> x0, matrix products: 12.6 us -> none  [the longest x2 9.43 us: complex_product(): jnp.matmul(row_blocks, expand(right_block), preferred_element_type=jnp.fl...]
    squeeze x4 -> x0, local copies, waits for them, and re-layouts: 5.9 us -> none  [the longest x1 3.57 us: per_device(): isolated = green_local[0]]
    select_n x1 -> x0, local copies, waits for them, and re-layouts: 4.75 us -> none  [per_device(): following = jnp.where(at_top, isolated, arrived)]
  transfers between devices with their start and end apart: 12 -> 0, of which waited for: 12 -> 0; matrix products, arithmetic and copies ran while one was open for 2% -> 0% of each run, Pallas kernels for 0% -> 0%
where the time goes in v1:
time: 108 us; the launch traced here: 107 us
  Pallas kernels  103 us (95%)
  local copies, waits for them, and re-layouts  3.56 us (3%)
    pallas_call x1, Pallas kernels, per_device(): pl.pallas_call(functools.partial(kernel, (layers, rows_of, energies, chun...  103 us

profile of v1, /device:TPU:9, one launch (start us, length us, event | category | flops | bytes accessed | tf_op | source)
XLA Modules:
  0.0 106.9 jit_solution(14682230655797144939)
XLA Ops:
  0.0 0.0 copy-start.1
  0.0 1.2 %copy.4 = bf16[48,8,2,384]{3,1,2,0:T(8,128)(2,1)S(1)} copy(bf16[48,8,2,384]{3,2,1,0:T(2,128)(2,1)} %bitcast.8) | data formatting | bytes 1179648
  1.2 0.2 copy-done.1
  1.4 0.0 copy-start
  1.5 0.8 reshape.12.g_ref
  2.2 0.2 copy-done
  2.4 103.3 %sweep.1 = bf16[2,6,64,768]{3,2,1,0:T(8,128)(2,1)S(1)} custom-call(bf16[2,6,64,768]{3,2,1,0:T(8,128)(2,1)S(1)} %reshape.12.g_ref, bf16[384,768]{1,0:T(8,128)(2,1)S(1)} %bitcast.6, bf16[384,384]{1,0:T(8,128)(2,1)S(1)} %bitcast.7), custom_call_target="tpu_custom_call" | custom-call | tf_op jit(solution)/shard_map/sweep/pallas_call | solution.py:275
  105.8 1.2 %reshape.15 = bf16[1,2,384,2,384]{4,3,2,1,0:T(2,128)(2,1)} reshape(bf16[2,6,64,768]{3,2,1,0:T(8,128)(2,1)S(1)} %sweep.1) | data formatting | bytes 2359296 | tf_op jit(solution)/shard_map/reshape | solution.py:305
Async XLA Ops:
  0.0 1.4 %copy-start.1 = (bf16[1,2,384,2,384]{4,3,2,1,0:T(2,128)(2,1)S(1)}, bf16[1,2,384,2,384]{4,3,2,1,0:T(2,128)(2,1)}, u32[]{:S(2)}) copy-start(bf16[1,2,384,2,384]{4,3,2,1,0:T(2,128)(2,1)} %param.3) | copy-start | bytes 3538948
  1.4 1.0 copy-start

commit v2 on v1

v2 whole, which is shorter than its diff:
```python
import functools

import jax
import jax.numpy as jnp
from jax import lax
from jax.experimental import pallas as pl
from jax.experimental.pallas import tpu as pltpu
from jax.sharding import PartitionSpec as P

MESH = pl.DeviceIdType.MESH
F32 = jnp.float32
BF16 = jnp.bfloat16


def routes(layers, energies, chunks):
    if layers == 4 and energies == 2:
        cut = chunks - chunks // 6
        return [
            (0, 0, chunks, (3, 2)),
            (1, 0, cut, (3, 1, 0, 2)),
            (1, cut, chunks, (3, 2)),
            (0, 0, chunks, (2, 3, 1)),
            (1, 0, chunks, (2, 0, 1)),
            (0, 0, chunks, (1, 0)),
            (1, 0, cut, (1, 3, 2, 0)),
            (1, cut, chunks, (1, 0)),
        ]
    return [(i, 0, chunks, (l, l - 1)) for l in range(layers - 1, 0, -1) for i in range(energies)]


def kernel(
    dims, streams, slots,
    g_ref, h_ref, c_ref, out_ref,
    fin, halo, relay, right, left, hops, total,
    fin_sem, halo_sem, relay_sem, out_send, halo_send, relay_send,
):
    layers, rows_of, energies, chunks, rows, size, group = dims
    blocks, deep = chunks // group, group * rows
    me = lax.axis_index("layer")
    d = lax.axis_index("energy")
    has_low, has_high = d > 0, d < rows_of - 1
    top = me == layers - 1

    pairs = sorted({tuple(sorted(p)) for _, _, _, path in streams for p in zip(path, path[1:])})
    barrier = pltpu.get_barrier_semaphore()
    count = has_low.astype(jnp.int32) + has_high.astype(jnp.int32)
    for l in range(layers):
        partners = [b if a == l else a for a, b in pairs if l in (a, b)]

        @pl.when(me == l)
        def _(partners=partners):
            for other in partners:
                pl.semaphore_signal(barrier, inc=1, device_id={"layer": other}, device_id_type=MESH)

        count = count + jnp.where(me == l, len(partners), 0)

    @pl.when(has_low)
    def _():
        pl.semaphore_signal(barrier, inc=1, device_id={"energy": d - 1}, device_id_type=MESH)

    @pl.when(has_high)
    def _():
        pl.semaphore_signal(barrier, inc=1, device_id={"energy": d + 1}, device_id_type=MESH)

    pl.semaphore_wait(barrier, count)

    def halo_copy(src, side, i, c):
        return pltpu.make_async_remote_copy(
            src_ref=src.at[i, c], dst_ref=halo.at[side, i, c],
            send_sem=halo_send.at[side, i, c], recv_sem=halo_sem.at[side, i, c],
            device_id={"energy": d + 1 if side == 0 else d - 1}, device_id_type=MESH,
        )

    def forward(src, i, c):
        @pl.when(has_high)
        def _():
            halo_copy(src, 0, i, c).start()

        @pl.when(has_low)
        def _():
            halo_copy(src, 1, i, c).start()

    def stream_copy(s, hop, c):
        i, _, _, path = streams[s]
        target = path[hop + 1]
        if hop == 0:
            src, send = out_ref.at[i, c], out_send.at[i, c]
        else:
            src, send = relay.at[slots[s], c], relay_send.at[slots[s], c]
        if hop == len(path) - 2:
            dst, recv = fin.at[i, c], fin_sem.at[i, c]
        else:
            dst, recv = relay.at[slots[s], c], relay_sem.at[slots[s], c]
        return pltpu.make_async_remote_copy(
            src_ref=src, dst_ref=dst, send_sem=send, recv_sem=recv,
            device_id={"layer": target}, device_id_type=MESH,
        )

    def pass_on(s, hop):
        def body(c, carry):
            stream_copy(s, hop - 1, c).wait_recv()
            stream_copy(s, hop, c).start()
            return carry

        lax.fori_loop(streams[s][1], streams[s][2], body, 0)

    @pl.when(top)
    def _():
        def body(c, carry):
            for i in range(energies):
                forward(g_ref, i, c)
            return carry

        lax.fori_loop(0, chunks, body, 0)
        fin[...] = g_ref[...]

    @pl.when(d == 0)
    def _():
        halo[0] = jnp.zeros_like(halo[0])

    @pl.when(d == rows_of - 1)
    def _():
        halo[1] = jnp.zeros_like(halo[1])

    hop_r, hop_i = h_ref[:, :size], h_ref[:, size:]
    hops[:size, :] = h_ref[...]
    hops[size:, :size] = -hop_i
    hops[size:, size:] = hop_r
    for i in range(energies):
        full = g_ref[i].reshape(size, 2 * size)
        total[i] = full.astype(F32)
        coupled = jnp.dot(full, hops[...], preferred_element_type=F32).astype(BF16)
        parts = [coupled[:, :size], coupled[:, size:]]
        for which in range(2):
            if which == 1:
                parts = [
                    jnp.dot(part, c_ref[...], preferred_element_type=F32).astype(BF16)
                    for part in parts
                ]
            for j in range(blocks):
                for part in range(2):
                    left[i, which, j, :, part * deep : (part + 1) * deep] = parts[part][
                        :, j * deep : (j + 1) * deep
                    ]
            flip_r, flip_i = parts[0].T, parts[1].T
            right[i, which, :size, :size] = flip_r
            right[i, which, :size, size:] = flip_i
            right[i, which, size:, :size] = -flip_i
            right[i, which, size:, size:] = flip_r

    def relays(when):
        for l in range(layers):
            jobs = [
                (s, hop)
                for s, (_, _, _, path) in enumerate(streams)
                for hop, node in enumerate(path[1:-1], 1)
                if node == l and (path[0] > l + 1 if when == "before" else path[0] <= l)
            ]
            if jobs:
                @pl.when(me == l)
                def _(jobs=jobs):
                    for s, hop in jobs:
                        pass_on(s, hop)

    relays("before")

    def add_block(i, which, j, value):
        mid = jnp.dot(value, right[i, which], preferred_element_type=F32).astype(BF16)
        swapped = jnp.concatenate([-mid[:, size:], mid[:, :size]], axis=1)
        both = jnp.concatenate([mid, swapped], axis=0)
        total[i] += jnp.dot(left[i, which, j], both, preferred_element_type=F32)

    def block_of(ref, j):
        return ref[pl.ds(j * group, group)].reshape(deep, 2 * size)

    lags = []
    for i in range(energies):
        lag = jnp.int32(0)
        for l in range(layers - 1):
            hops_of = {e: len(path) for e, lo, _, path in streams if path[-1] == l and lo == 0}
            late = 1 if hops_of[i] > min(hops_of.values()) else 0
            lag = lag + jnp.where(me == l, late, 0)
        lags.append(lag)
    worst = 1 if any(len(path) > 2 for _, _, _, path in streams) else 0

    def step(t, carry):
        for sub in range(group):
            for i in range(energies):
                j = t - lags[i]

                @pl.when((j >= 0) & (j < blocks) & jnp.logical_not(top))
                def _(i=i, j=j, sub=sub):
                    c = j * group + sub
                    pltpu.make_async_remote_copy(
                        src_ref=fin.at[i, c], dst_ref=fin.at[i, c],
                        send_sem=out_send.at[i, c], recv_sem=fin_sem.at[i, c],
                        device_id={"layer": me + 1}, device_id_type=MESH,
                    ).wait_recv()
                    forward(fin, i, c)

        for i in range(energies):
            j = t - lags[i]

            @pl.when((j >= 0) & (j < blocks))
            def _(i=i, j=j):
                add_block(i, 0, j, block_of(fin.at[i], j))

        for i in range(energies):
            j = t - lags[i] - 1

            @pl.when((j >= 0) & (j < blocks))
            def _(i=i, j=j):
                for sub in range(group):
                    @pl.when(has_low)
                    def _(sub=sub):
                        halo_copy(fin, 0, i, j * group + sub).wait_recv()

                    @pl.when(has_high)
                    def _(sub=sub):
                        halo_copy(fin, 1, i, j * group + sub).wait_recv()

                partner = block_of(halo.at[0, i], j).astype(F32) + block_of(
                    halo.at[1, i], j
                ).astype(F32)
                add_block(i, 1, j, partner.astype(BF16))

        return carry

    lax.fori_loop(0, blocks + 1 + worst, step, 0)

    def finish(c, carry):
        for i in reversed(range(energies)):
            out_ref[i, c] = total[i, pl.ds(pl.multiple_of(c * rows, 16), rows), :].astype(BF16)
            for s, (e, first, end, path) in enumerate(streams):
                if e == i:
                    @pl.when((me == path[0]) & (c >= first) & (c < end))
                    def _(s=s):
                        stream_copy(s, 0, c).start()
        return carry

    lax.fori_loop(0, chunks, finish, 0)
    relays("after")

    def drain(c, carry):
        for s, (_, first, end, path) in enumerate(streams):
            for hop, node in enumerate(path[:-1]):
                @pl.when((me == node) & (c >= first) & (c < end))
                def _(s=s, hop=hop):
                    stream_copy(s, hop, c).wait_send()
        for i in range(energies):
            @pl.when(has_high)
            def _(i=i):
                halo_copy(fin, 0, i, c).wait_send()

            @pl.when(has_low)
            def _(i=i):
                halo_copy(fin, 1, i, c).wait_send()
        return carry

    lax.fori_loop(0, chunks, drain, 0)


def per_device(green_local, hopping, coupling):
    _, energies, size, _, _ = green_local.shape
    layers, rows_of = lax.axis_size("layer"), lax.axis_size("energy")
    rows = 32 if size % 32 == 0 else 16
    chunks = size // rows
    group = 128 // rows if size % 128 == 0 else 1
    streams = routes(layers, energies, chunks)
    slots, relayed = {}, 0
    for s, (_, _, _, path) in enumerate(streams):
        if len(path) > 2:
            slots[s] = relayed
            relayed += 1
    relayed = max(relayed, 1)
    block = (energies, chunks, rows, 2 * size)
    sem = pltpu.SemaphoreType.DMA
    vmem = pl.BlockSpec(memory_space=pltpu.VMEM)
    result = pl.pallas_call(
        functools.partial(
            kernel, (layers, rows_of, energies, chunks, rows, size, group), streams, slots
        ),
        out_shape=jax.ShapeDtypeStruct(block, BF16),
        in_specs=[vmem] * 3,
        out_specs=vmem,
        scratch_shapes=[
            pltpu.VMEM(block, BF16),
            pltpu.VMEM((2,) + block, BF16),
            pltpu.VMEM((relayed,) + block[1:], BF16),
            pltpu.VMEM((energies, 2, 2 * size, 2 * size), BF16),
            pltpu.VMEM((energies, 2, chunks // group, size, 2 * group * rows), BF16),
            pltpu.VMEM((2 * size, 2 * size), BF16),
            pltpu.VMEM((energies, size, 2 * size), F32),
            sem((energies, chunks)),
            sem((2, energies, chunks)),
            sem((relayed, chunks)),
            sem((energies, chunks)),
            sem((2, energies, chunks)),
            sem((relayed, chunks)),
        ],
        compiler_params=pltpu.CompilerParams(
            collective_id=0, has_side_effects=True, vmem_limit_bytes=48 * 2**20
        ),
        name="sweep",
    )(
        green_local.reshape(block),
        hopping.reshape(size, 2 * size),
        coupling.reshape(size, size),
    )
    return result.reshape(green_local.shape)


def solution(mesh):
    placed = (
        P("layer", "energy", None, None, None),
        P("layer", None, None, None),
        P("layer", None, None),
    )
    return jax.shard_map(
        per_device,
        mesh=mesh,
        in_specs=placed,
        out_specs=P("layer", "energy", None, None, None),
        check_vma=False,
    )
```

time: 108 us -> 99.5 us (0.921)
  Pallas kernels: 103 us -> 95.8 us
    pallas_call x1, Pallas kernels: 103 us -> 95.8 us  [per_device(): pl.pallas_call(functools.partial(kernel, (layers, rows_of, energies, chun...]
where the time goes in v2:
time: 99.5 us; the launch traced here: 99.3 us
  Pallas kernels  95.8 us (96%)
  local copies, waits for them, and re-layouts  3.56 us (4%)
    pallas_call x1, Pallas kernels, per_device(): pl.pallas_call(functools.partial(kernel, (layers, rows_of, energies, chun...  95.8 us

profile of v2, /device:TPU:9, one launch (start us, length us, event | category | flops | bytes accessed | tf_op | source)
XLA Modules:
  0.0 99.3 jit_solution(1503327064107836169)
XLA Ops:
  0.0 0.0 copy-start.1
  0.0 1.2 %copy.4 = bf16[48,8,2,384]{3,1,2,0:T(8,128)(2,1)S(1)} copy(bf16[48,8,2,384]{3,2,1,0:T(2,128)(2,1)} %bitcast.8) | data formatting | bytes 1179648
  1.2 0.2 copy-done.1
  1.4 0.0 copy-start
  1.5 0.8 reshape.12.g_ref
  2.2 0.2 copy-done
  2.4 95.8 %sweep.1 = bf16[2,12,32,768]{3,2,1,0:T(8,128)(2,1)S(1)} custom-call(bf16[2,12,32,768]{3,2,1,0:T(8,128)(2,1)S(1)} %reshape.12.g_ref, bf16[384,768]{1,0:T(8,128)(2,1)S(1)} %bitcast.6, bf16[384,384]{1,0:T(8,128)(2,1)S(1)} %bitcast.7), custom_call_target="tpu_custom_call" | custom-call | tf_op jit(solution)/shard_map/sweep/pallas_call | solution.py:279
  98.2 1.2 %reshape.15 = bf16[1,2,384,2,384]{4,3,2,1,0:T(2,128)(2,1)} reshape(bf16[2,12,32,768]{3,2,1,0:T(8,128)(2,1)S(1)} %sweep.1) | data formatting | bytes 2359296 | tf_op jit(solution)/shard_map/reshape | solution.py:310
Async XLA Ops:
  0.0 1.4 %copy-start.1 = (bf16[1,2,384,2,384]{4,3,2,1,0:T(2,128)(2,1)S(1)}, bf16[1,2,384,2,384]{4,3,2,1,0:T(2,128)(2,1)}, u32[]{:S(2)}) copy-start(bf16[1,2,384,2,384]{4,3,2,1,0:T(2,128)(2,1)} %param.3) | copy-start | bytes 3538948
  1.4 1.0 copy-start

commit v3 on v2

--- a/solution.py
+++ b/solution.py
@@ -13,18 +13,6 @@
 
 
 def routes(layers, energies, chunks):
-    if layers == 4 and energies == 2:
-        cut = chunks - chunks // 6
-        return [
-            (0, 0, chunks, (3, 2)),
-            (1, 0, cut, (3, 1, 0, 2)),
-            (1, cut, chunks, (3, 2)),
-            (0, 0, chunks, (2, 3, 1)),
-            (1, 0, chunks, (2, 0, 1)),
-            (0, 0, chunks, (1, 0)),
-            (1, 0, cut, (1, 3, 2, 0)),
-            (1, cut, chunks, (1, 0)),
-        ]
     return [(i, 0, chunks, (l, l - 1)) for l in range(layers - 1, 0, -1) for i in range(energies)]
 
 
@@ -310,14 +298,441 @@
     return result.reshape(green_local.shape)
 
 
+def square_kernel(
+    dims,
+    g_ref, h_ref, c_ref, out_ref,
+    own, fin, halo, res, back, hop_in, cpl_in, right, left, hops, cpl, total,
+    fin_sem, halo_sem, back_sem, g_sem, hop_sem, cpl_sem,
+    fin_send, halo_send, back_send, g_send, hop_send, cpl_send,
+):
+    rows_of, chunks, rows, size, group = dims
+    blocks, deep = chunks // group, group * rows
+    parts_of_half = hop_in.shape[1]
+    me = lax.axis_index("layer")
+    d = lax.axis_index("energy")
+    has_low, has_high = d > 0, d < rows_of - 1
+    half = lax.rem(d, 2)
+    twin = d + 1 - 2 * half
+    first, even, odd, last = me == 3, me == 1, me == 2, me == 0
+    ends, middle = first | last, even | odd
+
+    barrier = pltpu.get_barrier_semaphore()
+    count = has_low.astype(jnp.int32) + has_high.astype(jnp.int32)
+    for l, partners in enumerate(((1, 2), (0, 2, 3), (0, 1, 3), (1, 2))):
+        @pl.when(me == l)
+        def _(partners=partners):
+            for other in partners:
+                pl.semaphore_signal(barrier, inc=1, device_id={"layer": other}, device_id_type=MESH)
+
+        count = count + jnp.where(me == l, len(partners), 0)
+
+    @pl.when(has_low)
+    def _():
+        pl.semaphore_signal(barrier, inc=1, device_id={"energy": d - 1}, device_id_type=MESH)
+
+    @pl.when(has_high)
+    def _():
+        pl.semaphore_signal(barrier, inc=1, device_id={"energy": d + 1}, device_id_type=MESH)
+
+    pl.semaphore_wait(barrier, count)
+
+    def remote(src, dst, send, recv, **where):
+        return pltpu.make_async_remote_copy(
+            src_ref=src, dst_ref=dst, send_sem=send, recv_sem=recv,
+            device_id=where, device_id_type=MESH,
+        )
+
+    def halo_copy(src, side, slot, c):
+        return remote(
+            src, halo.at[side, slot, c], halo_send.at[side, slot, c], halo_sem.at[side, slot, c],
+            energy=d + 1 if side == 0 else d - 1,
+        )
+
+    def forward(src, slot, c):
+        @pl.when(has_high)
+        def _():
+            halo_copy(src, 0, slot, c).start()
+
+        @pl.when(has_low)
+        def _():
+            halo_copy(src, 1, slot, c).start()
+
+    def result_copy(k, c, target, slot):
+        return remote(
+            res.at[k, c], fin.at[slot, c], fin_send.at[k, c], fin_sem.at[slot, c], layer=target
+        )
+
+    def back_copy(k, c, target):
+        return remote(res.at[k, c], back.at[c], back_send.at[c], back_sem.at[c], layer=target)
+
+    def block_copy(i, k, target):
+        return remote(g_ref.at[i], own.at[k], g_send, g_sem, layer=target)
+
+    def hop_copy(src, stage, side, q, **where):
+        return remote(
+            src.at[side, q], hop_in.at[side, q], hop_send.at[stage, q], hop_sem.at[side, q], **where
+        )
+
+    def cpl_copy(src, stage, side, **where):
+        return remote(src.at[side], cpl_in.at[side], cpl_send.at[stage], cpl_sem.at[side], **where)
+
+    def factors_to(target):
+        cpl_copy(c_ref, 0, half, layer=target).start()
+        for q in range(parts_of_half):
+            hop_copy(h_ref, 0, half, q, layer=target).start()
+
+    @pl.when(first)
+    def _():
+        def body(c, carry):
+            for k in range(2):
+                forward(g_ref.at[k, c], k, c)
+            return carry
+
+        lax.fori_loop(0, chunks, body, 0)
+        fin[...] = g_ref[...]
+
+    @pl.when(odd)
+    def _():
+        block_copy(0, 0, 1).start()
+        factors_to(0)
+        own[0] = g_ref[1]
+
+    @pl.when(even)
+    def _():
+        factors_to(2)
+        block_copy(1, 1, 2).start()
+        own[1] = g_ref[0]
+
+    @pl.when(ends)
+    def _():
+        own[...] = g_ref[...]
+
+    @pl.when(d == 0)
+    def _():
+        halo[0] = jnp.zeros_like(halo[0])
+
+    @pl.when(d == rows_of - 1)
+    def _():
+        halo[1] = jnp.zeros_like(halo[1])
+
+    @pl.when(last)
+    def _():
+        cpl_copy(cpl_in, 0, half, layer=1).wait_recv()
+        cpl_copy(cpl_in, 0, half, layer=1).start()
+        for q in range(parts_of_half):
+            hop_copy(hop_in, 0, half, q, layer=1).wait_recv()
+            hop_copy(hop_in, 0, half, q, layer=1).start()
+
+    def swap_halves():
+        cpl_copy(cpl_in, 1, half, energy=twin).wait_recv()
+        cpl_copy(cpl_in, 1, half, energy=twin).start()
+        for q in range(parts_of_half):
+            hop_copy(hop_in, 1, half, q, energy=twin).wait_recv()
+            hop_copy(hop_in, 1, half, q, energy=twin).start()
+        cpl_copy(cpl_in, 1, 1 - half, energy=twin).wait_recv()
+        for q in range(parts_of_half):
+            hop_copy(hop_in, 1, 1 - half, q, energy=twin).wait_recv()
+
+    def prepare(k, arrived):
+        def fill(hop_src, cpl_src):
+            whole = hop_src[...].reshape(size, 2 * size)
+            hops[:size, :] = whole
+            hops[size:, :size] = -whole[:, size:]
+            hops[size:, size:] = whole[:, :size]
+            cpl[...] = cpl_src[...].reshape(size, size)
+
+        @pl.when(arrived)
+        def _():
+            block_copy(0, k, 1).wait_recv()
+            fill(hop_in, cpl_in)
+
+        @pl.when(jnp.logical_not(arrived))
+        def _():
+            fill(h_ref, c_ref)
+
+        full = own[k].reshape(size, 2 * size)
+        total[k] = full.astype(F32)
+        coupled = jnp.dot(full, hops[...], preferred_element_type=F32).astype(BF16)
+        parts = [coupled[:, :size], coupled[:, size:]]
+        for which in range(2):
+            if which == 1:
+                parts = [
+                    jnp.dot(part, cpl[...], preferred_element_type=F32).astype(BF16)
+                    for part in parts
+                ]
+            for j in range(blocks):
+                for part in range(2):
+                    left[k, which, j, :, part * deep : (part + 1) * deep] = parts[part][
+                        :, j * deep : (j + 1) * deep
+                    ]
+            flip_r, flip_i = parts[0].T, parts[1].T
+            right[k, which, :size, :size] = flip_r
+            right[k, which, :size, size:] = flip_i
+            right[k, which, size:, :size] = -flip_i
+            right[k, which, size:, size:] = flip_r
+
+    def prepare_early(n, carry):
+        k = jnp.where(even, 1 - n, n)
+
+        @pl.when(even & (n == 1))
+        def _():
+            swap_halves()
+
+        @pl.when(jnp.logical_not(odd & (n == 1)))
+        def _():
+            prepare(k, even & (n == 1))
+
+        return carry
+
+    lax.fori_loop(0, 2, prepare_early, 0)
+
+    def add_block(k, which, j, value):
+        mid = jnp.dot(value, right[k, which], preferred_element_type=F32).astype(BF16)
+        swapped = jnp.concatenate([-mid[:, size:], mid[:, :size]], axis=1)
+        both = jnp.concatenate([mid, swapped], axis=0)
+        total[k] += jnp.dot(left[k, which, j], both, preferred_element_type=F32)
+
+    def block_of(ref, j):
+        return ref[pl.ds(j * group, group)].reshape(deep, 2 * size)
+
+    def arrive(slot, c):
+        result_copy(0, c, me, slot).wait_recv()
+        forward(fin.at[slot, c], slot, c)
+
+    def add_partner(k, j):
+        for sub in range(group):
+            c = j * group + sub
+
+            @pl.when(has_low)
+            def _(c=c):
+                halo_copy(fin.at[k, c], 0, k, c).wait_recv()
+
+            @pl.when(has_high)
+            def _(c=c):
+                halo_copy(fin.at[k, c], 1, k, c).wait_recv()
+
+        partner = block_of(halo.at[0, k], j).astype(F32) + block_of(halo.at[1, k], j).astype(F32)
+        add_block(k, 1, j, partner.astype(BF16))
+
+    def round_chunk(k, c):
+        res[k, c] = total[k, pl.ds(pl.multiple_of(c * rows, 16), rows), :].astype(BF16)
+
+    @pl.when(ends)
+    def _():
+        def step(t, carry):
+            @pl.when((t < blocks) & last)
+            def _():
+                for sub in range(group):
+                    for k in range(2):
+                        arrive(k, t * group + sub)
+
+            for k in range(2):
+                @pl.when(t < blocks)
+                def _(k=k):
+                    add_block(k, 0, t, block_of(fin.at[k], t))
+
+            for k in range(2):
+                @pl.when(t >= 1)
+                def _(k=k):
+                    add_partner(k, t - 1)
+
+            return carry
+
+        lax.fori_loop(0, blocks + 1, step, 0)
+
+        def finish(c, carry):
+            for k in range(2):
+                round_chunk(k, c)
+
+                @pl.when(first)
+                def _(k=k):
+                    result_copy(k, c, 1 + k, 0).start()
+            return carry
+
+        lax.fori_loop(0, chunks, finish, 0)
+        out_ref[...] = res[...]
+
+    @pl.when(middle)
+    def _():
+        @pl.when(odd)
+        def _():
+            swap_halves()
+
+        def step(t, carry):
+            @pl.when(t < blocks)
+            def _():
+                for sub in range(group):
+                    arrive(0, t * group + sub)
+                add_block(0, 0, t, block_of(fin.at[0], t))
+
+            @pl.when(t >= 1)
+            def _():
+                add_partner(0, t - 1)
+
+            return carry
+
+        lax.fori_loop(0, blocks + 1, step, 0)
+
+        def finish_two(c, carry):
+            round_chunk(0, c)
+            forward(res.at[0, c], 1, c)
+            return carry
+
+        lax.fori_loop(0, chunks, finish_two, 0)
+
+        @pl.when(even)
+        def _():
+            def body(c, carry):
+                back_copy(0, c, 2).start()
+                return carry
+
+            lax.fori_loop(0, chunks, body, 0)
+
+        @pl.when(odd)
+        def _():
+            prepare(1, odd)
+
+        def near(j, carry):
+            add_block(1, 0, j, block_of(res.at[0], j))
+            return carry
+
+        def far(j, carry):
+            add_partner(1, j)
+            return carry
+
+        lax.fori_loop(0, blocks, near, 0)
+        lax.fori_loop(0, blocks, far, 0)
+
+        def finish_one(c, carry):
+            round_chunk(1, c)
+            result_copy(1, c, 0, me - 1).start()
+            return carry
+
+        lax.fori_loop(0, chunks, finish_one, 0)
+
+        @pl.when(odd)
+        def _():
+            def body(c, carry):
+                back_copy(1, c, 1).start()
+                return carry
+
+            lax.fori_loop(0, chunks, body, 0)
+            out_ref[1] = res[0]
+
+        @pl.when(even)
+        def _():
+            out_ref[0] = res[1]
+
+        def home(c, carry):
+            back_copy(0, c, me).wait_recv()
+            out_ref[2 - me, c] = back[c]
+            return carry
+
+        lax.fori_loop(0, chunks, home, 0)
+
+    def drain(c, carry):
+        for k in range(2):
+            @pl.when(first | (middle & (k == 1)))
+            def _(k=k):
+                result_copy(k, c, me, 0).wait_send()
+
+            @pl.when(has_high)
+            def _(k=k):
+                halo_copy(fin.at[k, c], 0, k, c).wait_send()
+
+            @pl.when(has_low)
+            def _(k=k):
+                halo_copy(fin.at[k, c], 1, k, c).wait_send()
+
+        @pl.when(middle)
+        def _():
+            back_copy(0, c, me).wait_send()
+
+        return carry
+
+    lax.fori_loop(0, chunks, drain, 0)
+
+    @pl.when(middle)
+    def _():
+        block_copy(0, 0, me).wait_send()
+        cpl_copy(cpl_in, 1, half, energy=twin).wait_send()
+        for q in range(parts_of_half):
+            hop_copy(hop_in, 1, half, q, energy=twin).wait_send()
+
+    @pl.when(middle | last)
+    def _():
+        cpl_copy(cpl_in, 0, half, layer=me).wait_send()
+        for q in range(parts_of_half):
+            hop_copy(hop_in, 0, half, q, layer=me).wait_send()
+
+
+def square_sweep(green_local, hopping, coupling):
+    _, _, size, _, _ = green_local.shape
+    rows_of = lax.axis_size("energy")
+    rows = 32
+    chunks, group = size // rows, 128 // rows
+    block = (2, chunks, rows, 2 * size)
+    hop_block = (2, 2, size // 4, 2 * size)
+    cpl_block = (2, size // 2, size)
+    sem = pltpu.SemaphoreType.DMA
+    vmem = pl.BlockSpec(memory_space=pltpu.VMEM)
+    result = pl.pallas_call(
+        functools.partial(square_kernel, (rows_of, chunks, rows, size, group)),
+        out_shape=jax.ShapeDtypeStruct(block, BF16),
+        in_specs=[vmem] * 3,
+        out_specs=vmem,
+        scratch_shapes=[
+            pltpu.VMEM(block, BF16),
+            pltpu.VMEM(block, BF16),
+            pltpu.VMEM((2,) + block, BF16),
+            pltpu.VMEM(block, BF16),
+            pltpu.VMEM(block[1:], BF16),
+            pltpu.VMEM(hop_block, BF16),
+            pltpu.VMEM(cpl_block, BF16),
+            pltpu.VMEM((2, 2, 2 * size, 2 * size), BF16),
+            pltpu.VMEM((2, 2, chunks // group, size, 2 * group * rows), BF16),
+            pltpu.VMEM((2 * size, 2 * size), BF16),
+            pltpu.VMEM((size, size), BF16),
+            pltpu.VMEM((2, size, 2 * size), F32),
+            sem((2, chunks)),
+            sem((2, 2, chunks)),
+            sem((chunks,)),
+            sem,
+            sem(hop_block[:2]),
+            sem((2,)),
+            sem((2, chunks)),
+            sem((2, 2, chunks)),
+            sem((chunks,)),
+            sem,
+            sem((2, hop_block[1])),
+            sem((2,)),
+        ],
+        compiler_params=pltpu.CompilerParams(
+            collective_id=1, has_side_effects=True, vmem_limit_bytes=48 * 2**20
+        ),
+        name="square_sweep",
+    )(
+        green_local.reshape(block),
+        hopping.reshape(hop_block),
+        coupling.reshape(cpl_block),
+    )
+    return result.reshape(green_local.shape)
+
+
 def solution(mesh):
+    def step(green_local, hopping, coupling):
+        layers, rows_of = lax.axis_size("layer"), lax.axis_size("energy")
+        _, energies, size, _, _ = green_local.shape
+        square = layers == 4 and energies == 2 and rows_of % 2 == 0 and size % 128 == 0
+        return (square_sweep if square else per_device)(green_local, hopping, coupling)
+
     placed = (
         P("layer", "energy", None, None, None),
         P("layer", None, None, None),
         P("layer", None, None),
     )
     return jax.shard_map(
-        per_device,
+        step,
         mesh=mesh,
         in_specs=placed,
         out_specs=P("layer", "energy", None, None, None),

time: 99.5 us -> 76.7 us (0.77)
  Pallas kernels: 95.8 us -> 72.1 us
    pallas_call x1, Pallas kernels: 95.8 us -> 72.1 us  [square_sweep(): pl.pallas_call(functools.partial(square_kernel, (rows_of, chunks, rows, s...]
    reshape x2 -> x3, local copies, waits for them, and re-layouts: 1.93 us -> 4.16 us  [the longest x1 2.2 us: square_sweep(): hopping.reshape(hop_block)]
    unnamed x5 -> x4, local copies, waits for them, and re-layouts: 1.63 us -> 0.16 us
where the time goes in v3:
time: 76.7 us; the launch traced here: 76.5 us
  Pallas kernels  72.1 us (94%)
  local copies, waits for them, and re-layouts  4.32 us (6%)
    pallas_call x1, Pallas kernels, square_sweep(): pl.pallas_call(functools.partial(square_kernel, (rows_of, chunks, rows, s...  72.1 us
    reshape x1, local copies, waits for them, and re-layouts, square_sweep(): hopping.reshape(hop_block)  2.2 us

profile of v3, /device:TPU:9, one launch (start us, length us, event | category | flops | bytes accessed | tf_op | source)
XLA Modules:
  0.0 76.5 jit_solution(15505812308393228021)
XLA Ops:
  0.0 0.0 copy-start.1
  0.0 2.2 %reshape.13.h_ref = bf16[2,2,96,768]{3,2,1,0:T(8,128)(2,1)S(1)} reshape(bf16[1,384,2,384]{3,2,1,0:T(2,128)(2,1)} %param.4) | data formatting | bytes 1179648 | tf_op jit(solution)/shard_map/reshape | solution.py:716
  2.2 0.0 copy-done.1
  2.2 0.0 copy-start
  2.2 0.8 %reshape.12.g_ref = bf16[2,12,32,768]{3,2,1,0:T(8,128)(2,1)S(1)} reshape(bf16[1,2,384,2,384]{4,3,2,1,0:T(2,128)(2,1)S(1)} %copy-done.1) | data formatting | bytes 2359296 | tf_op jit(solution)/shard_map/reshape | solution.py:715
  3.0 0.2 copy-done
  3.2 72.1 %square_sweep.1 = bf16[2,12,32,768]{3,2,1,0:T(8,128)(2,1)S(1)} custom-call(bf16[2,12,32,768]{3,2,1,0:T(8,128)(2,1)S(1)} %reshape.12.g_ref, bf16[2,2,96,768]{3,2,1,0:T(8,128)(2,1)S(1)} %reshape.13.h_ref, bf16[2,192,384]{2,1,0:T(8,128)(2,1)S(1)} %bitcast.3), custom_call_target="tpu_custom_call" | custom-call | tf_op jit(solution)/shard_map/square_sweep/pallas_call | solution.py:679
  75.3 1.2 %reshape.15 = bf16[1,2,384,2,384]{4,3,2,1,0:T(2,128)(2,1)} reshape(bf16[2,12,32,768]{3,2,1,0:T(8,128)(2,1)S(1)} %square_sweep.1) | data formatting | bytes 2359296 | tf_op jit(solution)/shard_map/reshape | solution.py:719
Async XLA Ops:
  0.0 2.2 %copy-start.1 = (bf16[1,2,384,2,384]{4,3,2,1,0:T(2,128)(2,1)S(1)}, bf16[1,2,384,2,384]{4,3,2,1,0:T(2,128)(2,1)}, u32[]{:S(2)}) copy-start(bf16[1,2,384,2,384]{4,3,2,1,0:T(2,128)(2,1)} %param.3) | copy-start | bytes 3538948
  2.2 1.0 %copy-start = (bf16[1,384,384]{2,1,0:T(8,128)(2,1)S(1)}, bf16[1,384,384]{2,1,0:T(8,128)(2,1)}, u32[]{:S(2)}) copy-start(bf16[1,384,384]{2,1,0:T(8,128)(2,1)} %param.5) | copy-start | bytes 884740

commit v4 on v3

--- a/solution.py
+++ b/solution.py
@@ -301,13 +301,14 @@
 def square_kernel(
     dims,
     g_ref, h_ref, c_ref, out_ref,
-    own, fin, halo, res, back, hop_in, cpl_in, right, left, hops, cpl, total,
+    own, fin, halo, res, back, hop_in, cpl_in, right, left, hops, cpl, mid, total,
     fin_sem, halo_sem, back_sem, g_sem, hop_sem, cpl_sem,
     fin_send, halo_send, back_send, g_send, hop_send, cpl_send,
 ):
     rows_of, chunks, rows, size, group = dims
     blocks, deep = chunks // group, group * rows
-    parts_of_half = hop_in.shape[1]
+    parts_of_half = 2
+    hop_rows = size // (2 * parts_of_half)
     me = lax.axis_index("layer")
     d = lax.axis_index("energy")
     has_low, has_high = d > 0, d < rows_of - 1
@@ -369,8 +370,10 @@
         return remote(g_ref.at[i], own.at[k], g_send, g_sem, layer=target)
 
     def hop_copy(src, stage, side, q, **where):
+        start = pl.multiple_of((side * parts_of_half + q) * hop_rows, 16)
+        part = pl.ds(start, hop_rows)
         return remote(
-            src.at[side, q], hop_in.at[side, q], hop_send.at[stage, q], hop_sem.at[side, q], **where
+            src.at[part], hop_in.at[part], hop_send.at[stage, q], hop_sem.at[side, q], **where
         )
 
     def cpl_copy(src, stage, side, **where):
@@ -433,12 +436,17 @@
         for q in range(parts_of_half):
             hop_copy(hop_in, 1, 1 - half, q, energy=twin).wait_recv()
 
+    def expand(ref, start, value):
+        count, low = value.shape[0], start + size
+        if not isinstance(start, int):
+            start, low = pl.multiple_of(start, 16), pl.multiple_of(low, 16)
+        ref[pl.ds(start, count), :] = value
+        ref[pl.ds(low, count), :size] = -value[:, size:]
+        ref[pl.ds(low, count), size:] = value[:, :size]
+
     def prepare(k, arrived):
         def fill(hop_src, cpl_src):
-            whole = hop_src[...].reshape(size, 2 * size)
-            hops[:size, :] = whole
-            hops[size:, :size] = -whole[:, size:]
-            hops[size:, size:] = whole[:, :size]
+            expand(hops, 0, hop_src[...])
             cpl[...] = cpl_src[...].reshape(size, size)
 
         @pl.when(arrived)
@@ -451,7 +459,6 @@
             fill(h_ref, c_ref)
 
         full = own[k].reshape(size, 2 * size)
-        total[k] = full.astype(F32)
         coupled = jnp.dot(full, hops[...], preferred_element_type=F32).astype(BF16)
         parts = [coupled[:, :size], coupled[:, size:]]
         for which in range(2):
@@ -460,11 +467,8 @@
                     jnp.dot(part, cpl[...], preferred_element_type=F32).astype(BF16)
                     for part in parts
                 ]
-            for j in range(blocks):
-                for part in range(2):
-                    left[k, which, j, :, part * deep : (part + 1) * deep] = parts[part][
-                        :, j * deep : (j + 1) * deep
-                    ]
+            for part in range(2):
+                left[k, which, :, part * size : (part + 1) * size] = parts[part]
             flip_r, flip_i = parts[0].T, parts[1].T
             right[k, which, :size, :size] = flip_r
             right[k, which, :size, size:] = flip_i
@@ -486,11 +490,18 @@
 
     lax.fori_loop(0, 2, prepare_early, 0)
 
-    def add_block(k, which, j, value):
-        mid = jnp.dot(value, right[k, which], preferred_element_type=F32).astype(BF16)
-        swapped = jnp.concatenate([-mid[:, size:], mid[:, :size]], axis=1)
-        both = jnp.concatenate([mid, swapped], axis=0)
-        total[k] += jnp.dot(left[k, which, j], both, preferred_element_type=F32)
+    def near(k, ref):
+        value = jnp.dot(
+            ref[...].reshape(size, 2 * size), right[k, 0], preferred_element_type=F32
+        ).astype(BF16)
+        expand(hops, 0, value)
+        total[k] = own[k].reshape(size, 2 * size).astype(F32) + jnp.dot(
+            left[k, 0], hops[...], preferred_element_type=F32
+        )
+
+    def close(k):
+        value = total[k] + jnp.dot(left[k, 1], mid[k], preferred_element_type=F32)
+        res[k] = value.astype(BF16).reshape(chunks, rows, 2 * size)
 
     def block_of(ref, j):
         return ref[pl.ds(j * group, group)].reshape(deep, 2 * size)
@@ -512,13 +523,16 @@
                 halo_copy(fin.at[k, c], 1, k, c).wait_recv()
 
         partner = block_of(halo.at[0, k], j).astype(F32) + block_of(halo.at[1, k], j).astype(F32)
-        add_block(k, 1, j, partner.astype(BF16))
-
-    def round_chunk(k, c):
-        res[k, c] = total[k, pl.ds(pl.multiple_of(c * rows, 16), rows), :].astype(BF16)
+        value = jnp.dot(partner.astype(BF16), right[k, 1], preferred_element_type=F32)
+        expand(mid.at[k], j * deep, value.astype(BF16))
 
     @pl.when(ends)
     def _():
+        @pl.when(first)
+        def _():
+            for k in range(2):
+                near(k, fin.at[k])
+
         def step(t, carry):
             @pl.when((t < blocks) & last)
             def _():
@@ -526,30 +540,31 @@
                     for k in range(2):
                         arrive(k, t * group + sub)
 
-            for k in range(2):
-                @pl.when(t < blocks)
-                def _(k=k):
-                    add_block(k, 0, t, block_of(fin.at[k], t))
-
-            for k in range(2):
-                @pl.when(t >= 1)
-                def _(k=k):
+            @pl.when((t == blocks) & last)
+            def _():
+                for k in range(2):
+                    near(k, fin.at[k])
+
+            @pl.when(t >= 1)
+            def _():
+                for k in range(2):
                     add_partner(k, t - 1)
 
             return carry
 
         lax.fori_loop(0, blocks + 1, step, 0)
 
-        def finish(c, carry):
-            for k in range(2):
-                round_chunk(k, c)
-
-                @pl.when(first)
-                def _(k=k):
+        for k in range(2):
+            close(k)
+
+            @pl.when(first)
+            def _(k=k):
+                def body(c, carry):
                     result_copy(k, c, 1 + k, 0).start()
-            return carry
-
-        lax.fori_loop(0, chunks, finish, 0)
+                    return carry
+
+                lax.fori_loop(0, chunks, body, 0)
+
         out_ref[...] = res[...]
 
     @pl.when(middle)
@@ -563,7 +578,10 @@
             def _():
                 for sub in range(group):
                     arrive(0, t * group + sub)
-                add_block(0, 0, t, block_of(fin.at[0], t))
+
+            @pl.when(t == blocks)
+            def _():
+                near(0, fin.at[0])
 
             @pl.when(t >= 1)
             def _():
@@ -573,8 +591,9 @@
 
         lax.fori_loop(0, blocks + 1, step, 0)
 
+        close(0)
+
         def finish_two(c, carry):
-            round_chunk(0, c)
             forward(res.at[0, c], 1, c)
             return carry
 
@@ -592,19 +611,16 @@
         def _():
             prepare(1, odd)
 
-        def near(j, carry):
-            add_block(1, 0, j, block_of(res.at[0], j))
-            return carry
+        near(1, res.at[0])
 
         def far(j, carry):
             add_partner(1, j)
             return carry
 
-        lax.fori_loop(0, blocks, near, 0)
         lax.fori_loop(0, blocks, far, 0)
+        close(1)
 
         def finish_one(c, carry):
-            round_chunk(1, c)
             result_copy(1, c, 0, me - 1).start()
             return carry
 
@@ -672,7 +688,7 @@
     rows = 32
     chunks, group = size // rows, 128 // rows
     block = (2, chunks, rows, 2 * size)
-    hop_block = (2, 2, size // 4, 2 * size)
+    hop_block = (size, 2 * size)
     cpl_block = (2, size // 2, size)
     sem = pltpu.SemaphoreType.DMA
     vmem = pl.BlockSpec(memory_space=pltpu.VMEM)
@@ -690,21 +706,22 @@
             pltpu.VMEM(hop_block, BF16),
             pltpu.VMEM(cpl_block, BF16),
             pltpu.VMEM((2, 2, 2 * size, 2 * size), BF16),
-            pltpu.VMEM((2, 2, chunks // group, size, 2 * group * rows), BF16),
+            pltpu.VMEM((2, 2, size, 2 * size), BF16),
             pltpu.VMEM((2 * size, 2 * size), BF16),
             pltpu.VMEM((size, size), BF16),
+            pltpu.VMEM((2, 2 * size, 2 * size), BF16),
             pltpu.VMEM((2, size, 2 * size), F32),
             sem((2, chunks)),
             sem((2, 2, chunks)),
             sem((chunks,)),
             sem,
-            sem(hop_block[:2]),
+            sem((2, 2)),
             sem((2,)),
             sem((2, chunks)),
             sem((2, 2, chunks)),
             sem((chunks,)),
             sem,
-            sem((2, hop_block[1])),
+            sem((2, 2)),
             sem((2,)),
         ],
         compiler_params=pltpu.CompilerParams(

time: 76.7 us -> 75.4 us (0.983)
    reshape x1 -> x0, local copies, waits for them, and re-layouts: 2.2 us -> none  [square_sweep(): hopping.reshape(hop_block)]
    unnamed x4 -> x5, local copies, waits for them, and re-layouts: 0.16 us -> 1.63 us
where the time goes in v4:
time: 75.4 us; the launch traced here: 75.1 us
  Pallas kernels  71.6 us (95%)
  local copies, waits for them, and re-layouts  3.56 us (5%)
    pallas_call x1, Pallas kernels, square_sweep(): pl.pallas_call(functools.partial(square_kernel, (rows_of, chunks, rows, s...  71.6 us
    unnamed x5, local copies, waits for them, and re-layouts  1.63 us

profile of v4, /device:TPU:9, one launch (start us, length us, event | category | flops | bytes accessed | tf_op | source)
XLA Modules:
  0.0 75.1 jit_solution(7646141796505261916)
XLA Ops:
  0.0 0.0 copy-start.1
  0.0 1.2 %copy.4 = bf16[48,8,2,384]{3,1,2,0:T(8,128)(2,1)S(1)} copy(bf16[48,8,2,384]{3,2,1,0:T(2,128)(2,1)} %bitcast.8) | data formatting | bytes 1179648
  1.2 0.2 copy-done.1
  1.4 0.0 copy-start
  1.5 0.8 %reshape.12.g_ref = bf16[2,12,32,768]{3,2,1,0:T(8,128)(2,1)S(1)} reshape(bf16[1,2,384,2,384]{4,3,2,1,0:T(2,128)(2,1)S(1)} %copy-done.1) | data formatting | bytes 2359296 | tf_op jit(solution)/shard_map/reshape | solution.py:732
  2.2 0.2 copy-done
  2.4 71.6 %square_sweep.1 = bf16[2,12,32,768]{3,2,1,0:T(8,128)(2,1)S(1)} custom-call(bf16[2,12,32,768]{3,2,1,0:T(8,128)(2,1)S(1)} %reshape.12.g_ref, bf16[384,768]{1,0:T(8,128)(2,1)S(1)} %bitcast.6, bf16[2,192,384]{2,1,0:T(8,128)(2,1)S(1)} %bitcast.7), custom_call_target="tpu_custom_call" | custom-call | tf_op jit(solution)/shard_map/square_sweep/pallas_call | solution.py:695
  74.0 1.2 %reshape.15 = bf16[1,2,384,2,384]{4,3,2,1,0:T(2,128)(2,1)} reshape(bf16[2,12,32,768]{3,2,1,0:T(8,128)(2,1)S(1)} %square_sweep.1) | data formatting | bytes 2359296 | tf_op jit(solution)/shard_map/reshape | solution.py:736
Async XLA Ops:
  0.0 1.4 %copy-start.1 = (bf16[1,2,384,2,384]{4,3,2,1,0:T(2,128)(2,1)S(1)}, bf16[1,2,384,2,384]{4,3,2,1,0:T(2,128)(2,1)}, u32[]{:S(2)}) copy-start(bf16[1,2,384,2,384]{4,3,2,1,0:T(2,128)(2,1)} %param.3) | copy-start | bytes 3538948
  1.4 1.0 %copy-start = (bf16[1,384,384]{2,1,0:T(8,128)(2,1)S(1)}, bf16[1,384,384]{2,1,0:T(8,128)(2,1)}, u32[]{:S(2)}) copy-start(bf16[1,384,384]{2,1,0:T(8,128)(2,1)} %param.5) | copy-start | bytes 884740
